TPU v7x, 32 devices: a whole 2x2x4 slice. The times are simulated.
32 devices in a mesh: groups: 2 (over y), row: 4 (over x, core), col: 4 (over z).
Axes of the slice: x: 2, y: 2, z: 4, core: 2. Of those that a mesh axis runs over, the one named last changes fastest.
Arguments:
- object_slab: float32 [2, 2, 2048, 2048], P(None, None, ('groups', 'row'), 'col'), parts along dimension 2, may hold values from -5 to 5
- probe_field: float32 [4, 256, 256], P('groups'), parts along dimension 0, may hold values from -6 to 6
- prop_phase: float32 [256, 256], replicated, may hold values from -3.140625 to 3.140625
- intensities: float32 [16, 1024, 256], P(('groups', 'row'), 'col'), parts along dimension 0, may hold values from 0.1 to 3
- corners: int32 [32, 4, 2], P(('groups', 'row'), 'col'), parts along dimension 0, may hold values from 0 to 256, as said below
- slot_source: int32 [16, 4], P(('groups', 'row'), 'col'), parts along dimension 0, may hold values from 0 to 3, as said below
Outputs:
- updated_slab: float32 [2, 2, 2048, 2048], P(None, None, ('groups', 'row'), 'col'), parts along dimension 2
- updated_probe: float32 [4, 256, 256], P('groups'), parts along dimension 0
There are 2 independent parts, one for each index of `groups`. A program takes and returns all parts, laid end to end along the dimension named above; an argument that names none is the same for every part. Nothing has to cross between parts.
Inputs may be any that keep to these rules, and one draw needn't show every extreme that they name: `corners`: entry [t * 4 + d, c] gives the row and column, within tile (t, c), of the patch that scan owner d of column c may take from that tile; the row is below 256, the column at most 256. `slot_source`: entry [d * 2 + k, c] is the tile row of column c that holds slot k of scan owner (d, c); one owner's 2 entries differ; in each column no tile row is named more than 4 times, and some tile row exactly 4 times.
All inputs are finite; a program needn't handle non-finite values.
Results may differ from a plain program's by a relative error of at most 0.015.
The roundings to bfloat16 on the way count: a program that leaves them out, or rounds other values in their place, can miss the bound.
Values may be sent and summed in bfloat16 or wider, within the bound.
No kernel may reach another device: no remote copies, remote signals or barrier semaphores. Data moves between devices by JAX's collectives and lax.ppermute only.
A program may use at most 128 MiB of HBM per device.

v0:
```python
import functools

import jax
import jax.numpy as jnp
from jax import lax
from jax.experimental import pallas as pl
from jax.experimental.pallas import tpu as pltpu
from jax.sharding import PartitionSpec as P

step_object = 0.05
step_probe = 0.5
VMEM_BYTES = 48 * 1024 * 1024


def permute_pairs(block, axis, partner):
    return lax.ppermute(block, axis, [(i, partner(i)) for i in range(lax.axis_size(axis))])


def from_behind(block, axis, distance):
    devices = range(lax.axis_size(axis))
    route = [(i - distance, i) for i in devices if i - distance in devices]
    return lax.ppermute(block, axis, route)


def dft_tables(length):
    index = jnp.arange(length, dtype=jnp.int32)
    phase_index = index[:, None] * index[None, :] % length
    angles = phase_index.astype(jnp.float32) * (2.0 * jnp.pi / length)
    scale_factor = 1.0 / jnp.sqrt(jnp.float32(length))
    table_re = (jnp.cos(angles) * scale_factor).astype(jnp.bfloat16)
    table_im = (-jnp.sin(angles) * scale_factor).astype(jnp.bfloat16)
    first = jnp.concatenate(
        [jnp.concatenate([table_re, -table_im], 1), jnp.concatenate([table_im, table_re], 1)], 0
    )
    second = jnp.concatenate(
        [jnp.concatenate([table_re, table_im], 1), jnp.concatenate([-table_im, table_re], 1)], 0
    )
    return first, second


def product(a, b):
    return jnp.dot(a, b, preferred_element_type=jnp.float32)


def transform(fields, left_table, right_table):
    count = len(fields)
    n = fields[0][0].shape[0]
    stacked = jnp.concatenate(
        [
            jnp.concatenate([f[0].astype(jnp.bfloat16) for f in fields], 1),
            jnp.concatenate([f[1].astype(jnp.bfloat16) for f in fields], 1),
        ],
        0,
    )
    middle = product(left_table, stacked).astype(jnp.bfloat16)
    middle = jnp.concatenate(
        [
            jnp.concatenate([middle[:n, p * n : (p + 1) * n], middle[n:, p * n : (p + 1) * n]], 1)
            for p in range(count)
        ],
        0,
    )
    out = product(middle, right_table)
    return [(out[p * n : (p + 1) * n, :n], out[p * n : (p + 1) * n, n:]) for p in range(count)]


def one_hot_rows(shape, offset):
    rows = lax.broadcasted_iota(jnp.int32, shape, 0)
    columns = lax.broadcasted_iota(jnp.int32, shape, 1)
    return (columns == rows + offset).astype(jnp.bfloat16)


def one_hot_columns(shape, offset):
    rows = lax.broadcasted_iota(jnp.int32, shape, 0)
    columns = lax.broadcasted_iota(jnp.int32, shape, 1)
    return (rows == columns + offset).astype(jnp.bfloat16)


def cut(own_ref, rim_ref, n, corner_y, corner_x):
    height = own_ref.shape[1] + rim_ref.shape[1]
    width = own_ref.shape[2]
    planes = jnp.concatenate(
        [jnp.concatenate([own_ref[c], rim_ref[c]], 0) for c in range(2)], 1
    )
    rows = product(one_hot_rows((n, height), corner_y), planes).astype(jnp.bfloat16)
    rows = jnp.concatenate([rows[:, :width], rows[:, width:]], 0)
    both = product(rows, one_hot_columns((width, n), corner_x))
    return both[:n], both[n:]


def first_kernel(corner_ref, own_ref, rim_ref, probe_ref, kernel_ref, first_ref, second_ref, patch_ref, moved_ref):
    count, _, n, _ = patch_ref.shape
    base = pl.program_id(0) * count
    fronts = []
    for p in range(count):
        o_re, o_im = cut(own_ref, rim_ref, n, corner_ref[base + p, 0], corner_ref[base + p, 1])
        patch_ref[p, 0] = o_re.astype(jnp.bfloat16)
        patch_ref[p, 1] = o_im.astype(jnp.bfloat16)
        q_re, q_im = probe_ref[0], probe_ref[1]
        fronts.append((q_re * o_re - q_im * o_im, q_re * o_im + q_im * o_re))
    freq = transform(fronts, first_ref[...], second_ref[...])
    k_re, k_im = kernel_ref[0], kernel_ref[1]
    spread = [(k_re * r - k_im * i, k_re * i + k_im * r) for r, i in freq]
    moved = transform(spread, second_ref[...], first_ref[...])
    for p in range(count):
        moved_ref[p, 0] = moved[p][0]
        moved_ref[p, 1] = moved[p][1]


def second_kernel(
    corner_ref, own_ref, rim_ref, probe_ref, kernel_ref, first_ref, second_ref, patch_ref, moved_ref, *rest
):
    measured_refs = rest[:-3]
    grad_ref, probe_grad_ref, measured_ref = rest[-3:]
    count, _, n, _ = patch_ref.shape
    base = pl.program_id(0) * count

    @pl.when(pl.program_id(0) == 0)
    def _():
        for s, ref in enumerate(measured_refs):
            measured_ref[s] = ref[...]
        probe_grad_ref[...] = jnp.zeros_like(probe_grad_ref)

    seconds, slabs = [], []
    for p in range(count):
        o_re, o_im = cut(own_ref, rim_ref, n, corner_ref[base + p, 0], corner_ref[base + p, 1])
        m_re, m_im = moved_ref[p, 0], moved_ref[p, 1]
        slabs.append((o_re, o_im))
        seconds.append((m_re * o_re - m_im * o_im, m_re * o_im + m_im * o_re))
    far = transform(seconds, first_ref[...], second_ref[...])
    weighted = []
    for p, (f_re, f_im) in enumerate(far):
        measured = measured_ref[base + p].astype(jnp.float32)
        misfit = jnp.where(measured < 0.0, 0.0, f_re * f_re + f_im * f_im - measured)
        weighted.append((misfit * f_re, misfit * f_im))
    back_one = transform(weighted, second_ref[...], first_ref[...])
    carry = []
    for p, (b_re, b_im) in enumerate(back_one):
        m_re, m_im = moved_ref[p, 0], moved_ref[p, 1]
        o_re, o_im = slabs[p]
        grad_ref[p, 2] = (m_re * b_re + m_im * b_im).astype(jnp.bfloat16)
        grad_ref[p, 3] = (m_re * b_im - m_im * b_re).astype(jnp.bfloat16)
        carry.append((o_re * b_re + o_im * b_im, o_re * b_im - o_im * b_re))
    echo = transform(carry, first_ref[...], second_ref[...])
    k_re, k_im = kernel_ref[0], kernel_ref[1]
    undo = [(k_re * r + k_im * i, k_re * i - k_im * r) for r, i in echo]
    back_zero = transform(undo, second_ref[...], first_ref[...])
    total_re, total_im = probe_grad_ref[0], probe_grad_ref[1]
    q_re, q_im = probe_ref[0], probe_ref[1]
    for p, (b_re, b_im) in enumerate(back_zero):
        grad_ref[p, 0] = (q_re * b_re + q_im * b_im).astype(jnp.bfloat16)
        grad_ref[p, 1] = (q_re * b_im - q_im * b_re).astype(jnp.bfloat16)
        o_re = patch_ref[p, 0].astype(jnp.float32)
        o_im = patch_ref[p, 1].astype(jnp.float32)
        total_re += o_re * b_re + o_im * b_im
        total_im += o_re * b_im - o_im * b_re
    probe_grad_ref[0] = total_re
    probe_grad_ref[1] = total_im


def place_kernel(corner_ref, grad_ref, slab_ref, part_ref, rim_ref):
    positions, _, n, _ = grad_ref.shape
    height, width = slab_ref.shape[1:]
    wide = []
    for p in range(positions):
        move = one_hot_rows((n, width), corner_ref[p, 1])
        wide.append(product(grad_ref[p, 0], move).astype(jnp.bfloat16))
    wide = jnp.concatenate(wide, 0)
    tall = jnp.concatenate(
        [one_hot_columns((height + n, n), corner_ref[p, 0]) for p in range(positions)], 1
    )
    total = product(tall, wide)
    part_ref[0] = slab_ref[0] - step_object * total[:height]
    rim_ref[0] = total[height:].astype(jnp.bfloat16)


def whole(shape):
    return pl.BlockSpec(shape, lambda *_: (0,) * len(shape))


def per_position(shape):
    return pl.BlockSpec(shape, lambda i, *_: (i,) + (0,) * (len(shape) - 1))


def sum_everywhere(value):
    rows, n = value.shape
    row_count, col_count = lax.axis_size("row"), lax.axis_size("col")
    me = lax.axis_index("row")
    core, chip = me % 2, me // 2
    chips = row_count // 2
    half = rows // 2
    piece = half // chips
    send = lax.dynamic_slice_in_dim(value, (1 - core) * half, half, 0).astype(jnp.bfloat16)
    keep = lax.dynamic_slice_in_dim(value, core * half, half, 0)
    keep = keep + permute_pairs(send, "row", lambda i: i ^ 1).astype(jnp.float32)
    total = lax.dynamic_slice_in_dim(keep, chip * piece, piece, 0)
    for s in range(1, chips):
        send = lax.dynamic_slice_in_dim(keep, (chip ^ s) * piece, piece, 0).astype(jnp.bfloat16)
        total = total + permute_pairs(send, "row", lambda i: i ^ (2 * s)).astype(jnp.float32)
    send = total.astype(jnp.bfloat16)
    for s in range(1, col_count):
        total = total + permute_pairs(send, "col", lambda i: i ^ s).astype(jnp.float32)
    total = total.astype(jnp.bfloat16)
    gathered = jnp.zeros((half, n), jnp.bfloat16)
    gathered = lax.dynamic_update_slice_in_dim(gathered, total, chip * piece, 0)
    for s in range(1, chips):
        other = permute_pairs(total, "row", lambda i: i ^ (2 * s))
        gathered = lax.dynamic_update_slice_in_dim(gathered, other, (chip ^ s) * piece, 0)
    other = permute_pairs(gathered, "row", lambda i: i ^ 1)
    low = jnp.where(core == 0, gathered, other)
    high = jnp.where(core == 0, other, gathered)
    return jnp.concatenate([low, high], 0).astype(jnp.float32)


def per_device(object_slab, probe_field, prop_phase, intensities, corners, slot_source):
    slice_count, pair_count, height, width = object_slab.shape
    n = probe_field.shape[-1]
    row_count = lax.axis_size("row")
    col_count = lax.axis_size("col")
    slot_count = intensities.shape[0]
    me = lax.axis_index("row")
    first, second = dft_tables(n)
    kernel = jnp.stack([jnp.cos(prop_phase), jnp.sin(prop_phase)], 0)

    own = [object_slab[s].astype(jnp.bfloat16) for s in range(slice_count)]
    rim = [from_behind(block[:, :n], "row", -1) for block in own]

    sources = slot_source[:, 0]

    def message(target):
        hit = sources == target
        chosen = lax.dynamic_index_in_dim(intensities, jnp.argmax(hit), 0, keepdims=False)
        return jnp.where(jnp.any(hit), chosen, -1.0).astype(jnp.bfloat16)

    measured = [message(me)]
    origins = [me]
    for s in range(1, row_count):
        measured.append(permute_pairs(message(me ^ s), "row", lambda i: i ^ s))
        origins.append(me ^ s)
    spots = jnp.take(corners[:, 0], jnp.stack(origins), axis=0)

    count = 2
    steps = row_count // count
    plane = (2, n, n)
    patch_block = per_position((count, 2, n, n))
    table_specs = [whole((2 * n, 2 * n))] * 2
    tile_specs = [whole((pair_count, height, width)), whole((pair_count, n, width))]
    params = pltpu.CompilerParams(vmem_limit_bytes=VMEM_BYTES)
    unit = 2 * n * n * n
    patches, moved = pl.pallas_call(
        first_kernel,
        grid_spec=pltpu.PrefetchScalarGridSpec(
            num_scalar_prefetch=1,
            grid=(steps,),
            in_specs=tile_specs + [whole(plane)] * 2 + table_specs,
            out_specs=[patch_block, patch_block],
        ),
        out_shape=[
            jax.ShapeDtypeStruct((row_count, 2, n, n), jnp.bfloat16),
            jax.ShapeDtypeStruct((row_count, 2, n, n), jnp.float32),
        ],
        compiler_params=params,
        cost_estimate=pl.CostEstimate(flops=row_count * 28 * unit, bytes_accessed=6 * 2**20, transcendentals=0),
        name="first_half",
    )(spots, own[0], rim[0], probe_field, kernel, first, second)
    grads, probe_grad = pl.pallas_call(
        second_kernel,
        grid_spec=pltpu.PrefetchScalarGridSpec(
            num_scalar_prefetch=1,
            grid=(steps,),
            in_specs=tile_specs
            + [whole(plane)] * 2
            + table_specs
            + [patch_block, patch_block]
            + [whole((n, n))] * row_count,
            out_specs=[per_position((count, 4, n, n)), whole(plane)],
            scratch_shapes=[pltpu.VMEM((row_count, n, n), jnp.bfloat16)],
        ),
        out_shape=[
            jax.ShapeDtypeStruct((row_count, 4, n, n), jnp.bfloat16),
            jax.ShapeDtypeStruct(plane, jnp.float32),
        ],
        compiler_params=params,
        cost_estimate=pl.CostEstimate(flops=row_count * 44 * unit, bytes_accessed=8 * 2**20, transcendentals=0),
        name="second_half",
    )(spots, own[1], rim[1], probe_field, kernel, first, second, patches, moved, *measured)

    planes = slice_count * pair_count
    part, rim_grad = pl.pallas_call(
        place_kernel,
        grid_spec=pltpu.PrefetchScalarGridSpec(
            num_scalar_prefetch=1,
            grid=(planes,),
            in_specs=[
                pl.BlockSpec((row_count, 1, n, n), lambda i, *_: (0, i, 0, 0)),
                per_position((1, height, width)),
            ],
            out_specs=[per_position((1, height, width)), per_position((1, n, width))],
        ),
        out_shape=[
            jax.ShapeDtypeStruct((planes, height, width), jnp.float32),
            jax.ShapeDtypeStruct((planes, n, width), jnp.bfloat16),
        ],
        compiler_params=params,
        cost_estimate=pl.CostEstimate(flops=row_count * 24 * unit, bytes_accessed=7 * 2**20, transcendentals=0),
        name="place",
    )(spots, grads, object_slab.reshape(planes, height, width))
    total_probe = sum_everywhere(probe_grad.reshape(2 * n, n)).reshape(probe_field.shape)
    rim_grad = from_behind(rim_grad, "row", 1).astype(jnp.float32)
    updated_slab = part.at[:, :n].add(-step_object * rim_grad).reshape(object_slab.shape)
    updated_probe = probe_field - step_probe * total_probe / (row_count * col_count * slot_count)
    return (updated_slab, updated_probe)


def solution(mesh):
    placed = (
        P(None, None, ("groups", "row"), "col"),
        P("groups", None, None),
        P(),
        P(("groups", "row"), "col", None),
        P(("groups", "row"), "col", None),
        P(("groups", "row"), "col"),
    )
    return jax.shard_map(
        per_device,
        mesh=mesh,
        in_specs=placed,
        out_specs=(P(None, None, ("groups", "row"), "col"), P("groups", None, None)),
        check_vma=False,
    )
```

profile of v0, /device:TPU:0, one launch (start us, length us, event | category | flops | bytes accessed | tf_op | source)
XLA Modules:
  0.0 87.7 jit_solution(17298627462109800036)
XLA Ops:
  0.6 1.3 %bitcast_reduce_fusion.2 = (pred[]{:T(512)}, s32[]{:T(128)}) fusion(s32[2,1]{0,1:T(1,128)} %param.15, s32[]{:T(128)} %xor.16), kind=kLoop, calls=%fused_computation.49 | loop fusion | flops 9 | bytes 17 | tf_op jit(solution)/shard_map/per_device.<locals>.message/reduce | solution.py:232
  3.2 1.3 %bitcast_reduce_fusion.1 = (pred[]{:T(512)}, s32[]{:T(128)}) fusion(s32[2,1]{0,1:T(1,128)} %param.15, s32[]{:T(128)} %xor.17), kind=kLoop, calls=%fused_computation.48 | loop fusion | flops 9 | bytes 17 | tf_op jit(solution)/shard_map/per_device.<locals>.message/reduce | solution.py:232
  5.8 1.4 %compare_reduce_fusion = (pred[]{:T(512)}, pred[]{:T(512)}, pred[]{:T(512)}, pred[]{:T(512)}) fusion(s32[2,1]{0,1:T(1,128)} %param.15, s32[]{:T(128)} %xor.18, s32[]{:T(128)} %xor.16, s32[]{:T(128)} %axis_index.19, s32[]{:T(128)} %xor.17), kind=kLoop, calls=%fused_computation.52 | loop fusion | flops 12 | bytes 28 | tf_op jit(solution)/shard_map/reduce_or | solution.py:233
  7.2 1.3 %bitcast_reduce_fusion = (pred[]{:T(512)}, s32[]{:T(128)}) fusion(s32[2,1]{0,1:T(1,128)} %param.15, s32[]{:T(128)} %xor.18), kind=kLoop, calls=%fused_computation.47 | loop fusion | flops 9 | bytes 17 | tf_op jit(solution)/shard_map/per_device.<locals>.message/reduce | solution.py:232
  9.6 1.4 %bitcast_reduce_fusion.3 = (pred[]{:T(512)}, s32[]{:T(128)}) fusion(s32[2,1]{0,1:T(1,128)} %param.15, s32[]{:T(128)} %axis_index.19), kind=kLoop, calls=%fused_computation.50 | loop fusion | flops 9 | bytes 17 | tf_op jit(solution)/shard_map/per_device.<locals>.message/reduce | solution.py:232
  14.8 4.5 %fusion.11 = (bf16[256,256]{1,0:T(8,128)(2,1)}, bf16[256,256]{1,0:T(8,128)(2,1)}, bf16[256,256]{1,0:T(8,128)(2,1)S(1)}, bf16[256,256]{1,0:T(8,128)(2,1)}) fusion(f32[2,256,256]{2,1,0:T(8,128)} %param.13, s32[]{:T(128)S(6)} %select_n.144, pred[]{:T(512)} %get-tuple-element.42, s32[]{:T(128)S(6)} %select_n.138, pred[]{:T(512)} %get-tuple-element.43, ...), kind=kLoop, calls=%fused_computation.34 | loop fusion | flops 262144 | bytes 1048596 | tf_op jit(solution)/shard_map/convert_element_type | solution.py:233
  19.3 0.5 collective-permute-start.2
  19.8 2.5 %collective-permute-start.3 = (bf16[256,256]{1,0:T(8,128)(2,1)}, bf16[256,256]{1,0:T(8,128)(2,1)S(1)}, u32[]{:S(2)}, u32[]{:S(2)}) collective-permute-start(bf16[256,256]{1,0:T(8,128)(2,1)} %get-tuple-element.53), channel_id=1, source_target_pairs={{0,8},{4,12},{8,0},{12,4},{1,9},{5,13},{9,1},{13,5},{2,10},{6,14},... | collective-permute-start | bytes 393224 | tf_op jit(solution)/shard_map/ppermute | solution.py:16
  22.3 0.0 copy-start.2
  22.3 0.1 collective-permute-start.4
  22.4 1.7 %convert.4 = bf16[2,2,256,512]{3,2,1,0:T(8,128)(2,1)S(1)} convert(f32[2,2,256,512]{3,2,1,0:T(8,128)} %param.10) | non-fusion elementwise | flops 524288 | bytes 3145728 | tf_op jit(solution)/shard_map/convert.1
  24.1 0.0 copy-start.3
  24.2 0.1 slice_bitcast_fusion
  24.2 0.0 copy-start
  24.2 1.4 %collective-permute-start.1 = (bf16[2,256,512]{2,1,0:T(8,128)(2,1)S(1)}, bf16[2,256,512]{2,1,0:T(8,128)(2,1)}, u32[]{:S(2)}, u32[]{:S(2)}) collective-permute-start(bf16[2,256,512]{2,1,0:T(8,128)(2,1)S(1)} %get-tuple-element.48.own_ref), channel_id=1, source_target_pairs={{4,0},{8,4},{12,8},{5,1},{9,5},{13,9},{6,2},{10,6},{14,10},{7,3},{... | collective-permute-start | bytes 1572872 | tf_op jit(solution)/shard_map/ppermute | solution.py:22
  25.7 1.3 %collective-permute-start = (bf16[2,256,512]{2,1,0:T(8,128)(2,1)S(1)}, bf16[2,256,512]{2,1,0:T(8,128)(2,1)S(1)}, u32[]{:S(2)}, u32[]{:S(2)}) collective-permute-start(bf16[2,256,512]{2,1,0:T(8,128)(2,1)S(1)} %get-tuple-element.49.own_ref), channel_id=1, source_target_pairs={{4,0},{8,4},{12,8},{5,1},{9,5},{13,9},{6,2},{10,6},{14,10},{7,3},{... | collective-permute-start | bytes 1572872 | tf_op jit(solution)/shard_map/ppermute | solution.py:22
  27.0 1.1 %multiply_convert_fusion = (bf16[256,256]{1,0:T(8,128)(2,1)S(1)}, bf16[256,256]{1,0:T(8,128)(2,1)S(1)}) fusion(), kind=kLoop, calls=%fused_computation.24 | loop fusion | flops 1245184 | bytes 262144 | tf_op jit(solution)/shard_map/convert_element_type | solution.py:31
  28.1 0.1 fusion.14
  28.2 0.0 copy-done.2
  28.2 1.0 %cosine_bitcast_fusion = (f32[1,256,256]{2,1,0:T(8,128)S(1)}, f32[1,256,256]{2,1,0:T(8,128)S(1)}) fusion(f32[256,256]{1,0:T(8,128)S(1)} %copy-done.2), kind=kLoop, calls=%fused_computation.29 | loop fusion | bytes 786432 | tf_op jit(solution)/shard_map/stack | solution.py:223
  29.2 0.1 compare_and_fusion
  29.3 0.0 copy-done.3
  29.3 0.1 copy.8
  29.4 0.6 gather_fusion
  29.9 0.1 broadcast_select_fusion.2.corner_ref
  30.0 1.0 %fusion.13 = bf16[256,256]{1,0:T(8,128)(2,1)S(1)} fusion(), kind=kLoop, calls=%fused_computation.41 | loop fusion | flops 1310720 | bytes 131072 | tf_op jit(solution)/shard_map/neg | solution.py:33
  31.0 0.1 fusion.1
  31.1 0.0 collective-permute-done.1.rim_ref
  31.1 0.0 copy-done
  31.1 7.7 %first_half.1 = (bf16[4,2,256,256]{3,2,1,0:T(8,128)(2,1)S(1)}, f32[4,2,256,256]{3,2,1,0:T(8,128)}) custom-call(s32[4,2]{1,0:T(4,128)S(1)} %broadcast_select_fusion.2.corner_ref, bf16[2,256,512]{2,1,0:T(8,128)(2,1)S(1)} %get-tuple-element.48.own_ref, bf16[2,256,512]{2,1,0:T(8,128)(2,1)} %collective-permute-done.1.rim_ref, f32[2,256,256]{2,1,0:T(8,128)S(1)} %copy-done, ...), custom_call_target="tpu_custom_call" | custom-call | flops 3758096384 | bytes 6291456 | tf_op jit(solution)/shard_map/first_half/pallas_call | solution.py:250
  38.9 0.0 collective-permute-done.2.rest_1_
  38.9 0.0 collective-permute-done.3.rest_2_
  38.9 0.0 collective-permute-done.4.rest_3_
  38.9 0.0 collective-permute-done.rim_ref
  38.9 11.5 %second_half.1 = (bf16[4,4,256,256]{3,2,1,0:T(8,128)(2,1)}, f32[2,256,256]{2,1,0:T(8,128)S(1)}) custom-call(s32[4,2]{1,0:T(4,128)S(1)} %broadcast_select_fusion.2.corner_ref, bf16[2,256,512]{2,1,0:T(8,128)(2,1)S(1)} %get-tuple-element.49.own_ref, bf16[2,256,512]{2,1,0:T(8,128)(2,1)S(1)} %collective-permute-done.rim_ref, f32[2,256,256]{2,1,0:T(8,128)S(1)} %copy-done, ...), custom_call_target="tpu_custom_call" | custom-call | flops 5905580032 | bytes 8388608 | tf_op jit(solution)/shard_map/second_half/pallas_call | solution.py:266
  50.5 4.1 %collective-permute-start.6 = (bf16[256,256]{1,0:T(8,128)(2,1)S(1)}, bf16[256,256]{1,0:T(8,128)(2,1)S(1)}, u32[]{:S(2)}, u32[]{:S(2)}) collective-permute-start(bf16[256,256]{1,0:T(8,128)(2,1)S(1)} %dynamic-slice_convert_fusion), channel_id=1, source_target_pairs={{0,4},{4,0},{8,12},{12,8},{1,5},{5,1},{9,13},{13,9},{2,6},{6,2},{1... | collective-permute-start | bytes 393224 | tf_op jit(solution)/shard_map/ppermute | solution.py:16
  54.5 1.0 %collective-permute-done.6 = bf16[256,256]{1,0:T(8,128)(2,1)S(1)} collective-permute-done((bf16[256,256]{1,0:T(8,128)(2,1)S(1)}, bf16[256,256]{1,0:T(8,128)(2,1)S(1)}, u32[]{:S(2)}, u32[]{:S(2)}) %collective-permute-start.6) | collective-permute-done | bytes 131104 | tf_op jit(solution)/shard_map/ppermute | solution.py:16
  55.6 0.1 collective-permute-start.7
  55.6 0.0 copy-start.1
  55.6 1.6 %copy-done.1 = bf16[4,4,256,256]{3,2,1,0:T(8,128)(2,1)S(1)} copy-done((bf16[4,4,256,256]{3,2,1,0:T(8,128)(2,1)S(1)}, bf16[4,4,256,256]{3,2,1,0:T(8,128)(2,1)}, u32[]{:S(2)}) %copy-start.1) | copy-done | bytes 2097176
  57.2 6.6 %place.1 = (f32[4,256,512]{2,1,0:T(8,128)S(1)}, bf16[4,256,512]{2,1,0:T(8,128)(2,1)}) custom-call(s32[4,2]{1,0:T(4,128)S(1)} %broadcast_select_fusion.2.corner_ref, bf16[4,4,256,256]{3,2,1,0:T(8,128)(2,1)S(1)} %copy-done.1, f32[4,256,512]{2,1,0:T(8,128)} %bitcast.42), custom_call_target="tpu_custom_call" | custom-call | flops 3221225472 | bytes 7340032 | tf_op jit(solution)/shard_map/place/pallas_call | solution.py:289
  63.8 3.3 %collective-permute-start.5 = (bf16[4,256,512]{2,1,0:T(8,128)(2,1)}, bf16[4,256,512]{2,1,0:T(8,128)(2,1)}, u32[]{:S(2)}, u32[]{:S(2)}) collective-permute-start(bf16[4,256,512]{2,1,0:T(8,128)(2,1)} %get-tuple-element.40), channel_id=1, source_target_pairs={{0,4},{4,8},{8,12},{1,5},{5,9},{9,13},{2,6},{6,10},{10,14},{3,7},{... | collective-permute-start | bytes 3145736 | tf_op jit(solution)/shard_map/ppermute | solution.py:22
  67.0 0.0 collective-permute-done.7
  67.1 4.0 %collective-permute-start.10 = (bf16[128,256]{1,0:T(8,128)(2,1)S(1)}, bf16[128,256]{1,0:T(8,128)(2,1)S(1)}, u32[]{:S(2)}, u32[]{:S(2)}) collective-permute-start(bf16[128,256]{1,0:T(8,128)(2,1)S(1)} %fusion.12), channel_id=1, source_target_pairs={{0,3},{1,2},{2,1},{3,0},{4,7},{5,6},{6,5},{7,4},{8,11},{9,10},{10,... | collective-permute-start | bytes 196616 | tf_op jit(solution)/shard_map/ppermute | solution.py:16
  71.1 0.0 collective-permute-start.8
  71.1 0.6 collective-permute-start.9
  71.7 2.3 %collective-permute-done.10 = bf16[128,256]{1,0:T(8,128)(2,1)S(1)} collective-permute-done((bf16[128,256]{1,0:T(8,128)(2,1)S(1)}, bf16[128,256]{1,0:T(8,128)(2,1)S(1)}, u32[]{:S(2)}, u32[]{:S(2)}) %collective-permute-start.10) | collective-permute-done | bytes 65568 | tf_op jit(solution)/shard_map/ppermute | solution.py:16
  74.0 2.8 %collective-permute-done.8 = bf16[128,256]{1,0:T(8,128)(2,1)S(1)} collective-permute-done((bf16[128,256]{1,0:T(8,128)(2,1)S(1)}, bf16[128,256]{1,0:T(8,128)(2,1)S(1)}, u32[]{:S(2)}, u32[]{:S(2)}) %collective-permute-start.8) | collective-permute-done | bytes 65568 | tf_op jit(solution)/shard_map/ppermute | solution.py:16
  76.8 1.1 %collective-permute-done.9 = bf16[128,256]{1,0:T(8,128)(2,1)S(1)} collective-permute-done((bf16[128,256]{1,0:T(8,128)(2,1)S(1)}, bf16[128,256]{1,0:T(8,128)(2,1)S(1)}, u32[]{:S(2)}, u32[]{:S(2)}) %collective-permute-start.9) | collective-permute-done | bytes 65568 | tf_op jit(solution)/shard_map/ppermute | solution.py:16
  78.0 0.1 collective-permute-start.11
  78.1 4.3 %collective-permute-done.11 = bf16[128,256]{1,0:T(8,128)(2,1)S(1)} collective-permute-done((bf16[128,256]{1,0:T(8,128)(2,1)S(1)}, bf16[128,256]{1,0:T(8,128)(2,1)S(1)}, u32[]{:S(2)}, u32[]{:S(2)}) %collective-permute-start.11) | collective-permute-done | bytes 65568 | tf_op jit(solution)/shard_map/ppermute | solution.py:16
  82.4 0.1 collective-permute-start.12
  82.5 1.3 %collective-permute-done.12 = bf16[256,256]{1,0:T(8,128)(2,1)S(1)} collective-permute-done((bf16[256,256]{1,0:T(8,128)(2,1)S(1)}, bf16[256,256]{1,0:T(8,128)(2,1)S(1)}, u32[]{:S(2)}, u32[]{:S(2)}) %collective-permute-start.12) | collective-permute-done | bytes 131104 | tf_op jit(solution)/shard_map/ppermute | solution.py:16
  83.9 0.9 sub.12
  84.7 0.0 collective-permute-done.5
  84.7 3.0 %multiply_add_fusion = f32[4,256,512]{2,1,0:T(8,128)} fusion(f32[4,256,512]{2,1,0:T(8,128)S(1)} %get-tuple-element.39, bf16[4,256,512]{2,1,0:T(8,128)(2,1)} %collective-permute-done.5), kind=kLoop, calls=%fused_computation.1 | loop fusion | flops 1572864 | bytes 5242880 | tf_op jit(solution)/shard_map/add | solution.py:310
  (11 shorter events, 0.2 us)
Async XLA Ops:
  19.3 19.5 %collective-permute-start.2 = (bf16[256,256]{1,0:T(8,128)(2,1)}, bf16[256,256]{1,0:T(8,128)(2,1)S(1)}, u32[]{:S(2)}, u32[]{:S(2)}) collective-permute-start(bf16[256,256]{1,0:T(8,128)(2,1)} %get-tuple-element.51), channel_id=1, source_target_pairs={{0,4},{4,0},{8,12},{12,8},{1,5},{5,1},{9,13},{13,9},{2,6},{6,2},{1... | collective-permute-start | bytes 393224 | tf_op jit(solution)/shard_map/ppermute | solution.py:16
  19.8 19.1 %collective-permute-start.3 = (bf16[256,256]{1,0:T(8,128)(2,1)}, bf16[256,256]{1,0:T(8,128)(2,1)S(1)}, u32[]{:S(2)}, u32[]{:S(2)}) collective-permute-start(bf16[256,256]{1,0:T(8,128)(2,1)} %get-tuple-element.53), channel_id=1, source_target_pairs={{0,8},{4,12},{8,0},{12,4},{1,9},{5,13},{9,1},{13,5},{2,10},{6,14},... | collective-permute-start | bytes 393224 | tf_op jit(solution)/shard_map/ppermute | solution.py:16
  22.3 5.9 %copy-start.2 = (f32[256,256]{1,0:T(8,128)S(1)}, f32[256,256]{1,0:T(8,128)}, u32[]{:S(2)}) copy-start(f32[256,256]{1,0:T(8,128)} %param.12) | copy-start | bytes 786436
  22.3 16.6 %collective-permute-start.4 = (bf16[256,256]{1,0:T(8,128)(2,1)}, bf16[256,256]{1,0:T(8,128)(2,1)S(1)}, u32[]{:S(2)}, u32[]{:S(2)}) collective-permute-start(bf16[256,256]{1,0:T(8,128)(2,1)} %get-tuple-element.50), channel_id=1, source_target_pairs={{0,12},{4,8},{8,4},{12,0},{1,13},{5,9},{9,5},{13,1},{2,14},{6,10},... | collective-permute-start | bytes 393224 | tf_op jit(solution)/shard_map/ppermute | solution.py:16
  24.1 5.2 %copy-start.3 = (s32[4,1,2]{0,2,1:T(2,128)S(1)}, s32[4,1,2]{0,2,1:T(2,128)}, u32[]{:S(2)}) copy-start(s32[4,1,2]{0,2,1:T(2,128)} %param.14) | copy-start | bytes 100
  24.2 6.9 %copy-start = (f32[2,256,256]{2,1,0:T(8,128)S(1)}, f32[2,256,256]{2,1,0:T(8,128)}, u32[]{:S(2)}) copy-start(f32[2,256,256]{2,1,0:T(8,128)} %probe_ref.3) | copy-start | bytes 1572868
  24.2 6.9 %collective-permute-start.1 = (bf16[2,256,512]{2,1,0:T(8,128)(2,1)S(1)}, bf16[2,256,512]{2,1,0:T(8,128)(2,1)}, u32[]{:S(2)}, u32[]{:S(2)}) collective-permute-start(bf16[2,256,512]{2,1,0:T(8,128)(2,1)S(1)} %get-tuple-element.48.own_ref), channel_id=1, source_target_pairs={{4,0},{8,4},{12,8},{5,1},{9,5},{13,9},{6,2},{10,6},{14,10},{7,3},{... | collective-permute-start | bytes 1572872 | tf_op jit(solution)/shard_map/ppermute | solution.py:22
  25.7 13.2 %collective-permute-start = (bf16[2,256,512]{2,1,0:T(8,128)(2,1)S(1)}, bf16[2,256,512]{2,1,0:T(8,128)(2,1)S(1)}, u32[]{:S(2)}, u32[]{:S(2)}) collective-permute-start(bf16[2,256,512]{2,1,0:T(8,128)(2,1)S(1)} %get-tuple-element.49.own_ref), channel_id=1, source_target_pairs={{4,0},{8,4},{12,8},{5,1},{9,5},{13,9},{6,2},{10,6},{14,10},{7,3},{... | collective-permute-start | bytes 1572872 | tf_op jit(solution)/shard_map/ppermute | solution.py:22
  50.5 5.0 %collective-permute-start.6 = (bf16[256,256]{1,0:T(8,128)(2,1)S(1)}, bf16[256,256]{1,0:T(8,128)(2,1)S(1)}, u32[]{:S(2)}, u32[]{:S(2)}) collective-permute-start(bf16[256,256]{1,0:T(8,128)(2,1)S(1)} %dynamic-slice_convert_fusion), channel_id=1, source_target_pairs={{0,4},{4,0},{8,12},{12,8},{1,5},{5,1},{9,13},{13,9},{2,6},{6,2},{1... | collective-permute-start | bytes 393224 | tf_op jit(solution)/shard_map/ppermute | solution.py:16
  55.6 11.5 %collective-permute-start.7 = (bf16[128,256]{1,0:T(8,128)(2,1)S(1)}, bf16[128,256]{1,0:T(8,128)(2,1)S(1)}, u32[]{:S(2)}, u32[]{:S(2)}) collective-permute-start(bf16[128,256]{1,0:T(8,128)(2,1)S(1)} %dynamic-slice_convert_fusion.1), channel_id=1, source_target_pairs={{0,8},{4,12},{8,0},{12,4},{1,9},{5,13},{9,1},{13,5},{2,10},{6,14},... | collective-permute-start | bytes 196616 | tf_op jit(solution)/shard_map/ppermute | solution.py:16
  55.6 1.6 %copy-start.1 = (bf16[4,4,256,256]{3,2,1,0:T(8,128)(2,1)S(1)}, bf16[4,4,256,256]{3,2,1,0:T(8,128)(2,1)}, u32[]{:S(2)}) copy-start(bf16[4,4,256,256]{3,2,1,0:T(8,128)(2,1)} %get-tuple-element.38.grad_ref) | copy-start | bytes 6291460
  63.8 20.9 %collective-permute-start.5 = (bf16[4,256,512]{2,1,0:T(8,128)(2,1)}, bf16[4,256,512]{2,1,0:T(8,128)(2,1)}, u32[]{:S(2)}, u32[]{:S(2)}) collective-permute-start(bf16[4,256,512]{2,1,0:T(8,128)(2,1)} %get-tuple-element.40), channel_id=1, source_target_pairs={{0,4},{4,8},{8,12},{1,5},{5,9},{9,13},{2,6},{6,10},{10,14},{3,7},{... | collective-permute-start | bytes 3145736 | tf_op jit(solution)/shard_map/ppermute | solution.py:22
  67.1 6.9 %collective-permute-start.10 = (bf16[128,256]{1,0:T(8,128)(2,1)S(1)}, bf16[128,256]{1,0:T(8,128)(2,1)S(1)}, u32[]{:S(2)}, u32[]{:S(2)}) collective-permute-start(bf16[128,256]{1,0:T(8,128)(2,1)S(1)} %fusion.12), channel_id=1, source_target_pairs={{0,3},{1,2},{2,1},{3,0},{4,7},{5,6},{6,5},{7,4},{8,11},{9,10},{10,... | collective-permute-start | bytes 196616 | tf_op jit(solution)/shard_map/ppermute | solution.py:16
  71.1 5.8 %collective-permute-start.8 = (bf16[128,256]{1,0:T(8,128)(2,1)S(1)}, bf16[128,256]{1,0:T(8,128)(2,1)S(1)}, u32[]{:S(2)}, u32[]{:S(2)}) collective-permute-start(bf16[128,256]{1,0:T(8,128)(2,1)S(1)} %fusion.12), channel_id=1, source_target_pairs={{0,1},{1,0},{2,3},{3,2},{4,5},{5,4},{6,7},{7,6},{8,9},{9,8},{10,11... | collective-permute-start | bytes 196616 | tf_op jit(solution)/shard_map/ppermute | solution.py:16
  71.1 6.9 %collective-permute-start.9 = (bf16[128,256]{1,0:T(8,128)(2,1)S(1)}, bf16[128,256]{1,0:T(8,128)(2,1)S(1)}, u32[]{:S(2)}, u32[]{:S(2)}) collective-permute-start(bf16[128,256]{1,0:T(8,128)(2,1)S(1)} %fusion.12), channel_id=1, source_target_pairs={{0,2},{1,3},{2,0},{3,1},{4,6},{5,7},{6,4},{7,5},{8,10},{9,11},{10,... | collective-permute-start | bytes 196616 | tf_op jit(solution)/shard_map/ppermute | solution.py:16
  78.0 4.3 %collective-permute-start.11 = (bf16[128,256]{1,0:T(8,128)(2,1)S(1)}, bf16[128,256]{1,0:T(8,128)(2,1)S(1)}, u32[]{:S(2)}, u32[]{:S(2)}) collective-permute-start(bf16[128,256]{1,0:T(8,128)(2,1)S(1)} %get-tuple-element.47), channel_id=1, source_target_pairs={{0,8},{4,12},{8,0},{12,4},{1,9},{5,13},{9,1},{13,5},{2,10},{6,14},... | collective-permute-start | bytes 196616 | tf_op jit(solution)/shard_map/ppermute | solution.py:16
  82.4 1.4 %collective-permute-start.12 = (bf16[256,256]{1,0:T(8,128)(2,1)S(1)}, bf16[256,256]{1,0:T(8,128)(2,1)S(1)}, u32[]{:S(2)}, u32[]{:S(2)}) collective-permute-start(bf16[256,256]{1,0:T(8,128)(2,1)S(1)} %constant_dynamic-update-slice_fusion), channel_id=1, source_target_pairs={{0,4},{4,0},{8,12},{12,8},{1,5},{5,1},{9,13},{13,9},{2,6},{6,2},{1... | collective-permute-start | bytes 393224 | tf_op jit(solution)/shard_map/ppermute | solution.py:16
where the time goes:
time: 88.3 us; the launch traced here: 87.7 us
  Pallas kernels  25.8 us (29%)
  other arithmetic  19.4 us (22%)
  starting transfers between devices  18 us (20%)
  waiting for transfers between devices  12.8 us (14%)
  between operations  8.31 us (9%)
  local copies, waits for them, and re-layouts  3.34 us (4%)
    ppermute x10, waiting for transfers between devices, permute_pairs(): lax.ppermute(block, axis, [(i, partner(i)) for i in range(lax.axis_size(a...  12.8 us
    ppermute x10, starting transfers between devices, permute_pairs(): lax.ppermute(block, axis, [(i, partner(i)) for i in range(lax.axis_size(a...  12 us
    pallas_call x1, Pallas kernels, per_device(): pl.pallas_call(second_kernel, grid_spec=pltpu.PrefetchScalarGridSpec(num_...  11.5 us
    pallas_call x1, Pallas kernels, per_device(): pl.pallas_call(first_kernel, grid_spec=pltpu.PrefetchScalarGridSpec(num_s...  7.73 us
    pallas_call x1, Pallas kernels, per_device(): pl.pallas_call(place_kernel, grid_spec=pltpu.PrefetchScalarGridSpec(num_s...  6.56 us
    ppermute x3, starting transfers between devices, from_behind(): return lax.ppermute(block, axis, route)  5.97 us
    another operation x4, other arithmetic, message(): jnp.argmax(hit)  5.34 us
    convert_element_type x1, other arithmetic, message(): return jnp.where(jnp.any(hit), chosen, -1.0).astype(jnp.bfloat16)  4.49 us
  transfers between devices with their start and end apart: 13, of which 6 were waited for; matrix products, arithmetic and copies ran while one was open for 8% of the time, Pallas kernels for 16%

commit v1 on v0

--- a/solution.py
+++ b/solution.py
@@ -88,12 +88,32 @@
     return both[:n], both[n:]
 
 
-def first_kernel(corner_ref, own_ref, rim_ref, probe_ref, kernel_ref, first_ref, second_ref, patch_ref, moved_ref):
+def spot(me_ref, corner_ref, position):
+    owner = me_ref[0] ^ position
+    return corner_ref[owner, 0], corner_ref[owner, 1]
+
+
+def first_prep_kernel(slab_ref, own_ref):
+    own_ref[...] = slab_ref[...].astype(jnp.bfloat16)
+
+
+def second_prep_kernel(me_ref, source_ref, slab_ref, intensity_ref, own_ref, *message_refs):
+    own_ref[...] = slab_ref[...].astype(jnp.bfloat16)
+    for s, message_ref in enumerate(message_refs):
+        target = me_ref[0] ^ s
+        slot = jnp.int32(-1)
+        for k in range(intensity_ref.shape[0]):
+            slot = jnp.where(source_ref[k] == target, k, slot)
+        chosen = intensity_ref[jnp.maximum(slot, 0)]
+        message_ref[...] = jnp.where(slot >= 0, chosen, -1.0).astype(jnp.bfloat16)
+
+
+def first_kernel(me_ref, corner_ref, own_ref, rim_ref, probe_ref, kernel_ref, first_ref, second_ref, patch_ref, moved_ref):
     count, _, n, _ = patch_ref.shape
     base = pl.program_id(0) * count
     fronts = []
     for p in range(count):
-        o_re, o_im = cut(own_ref, rim_ref, n, corner_ref[base + p, 0], corner_ref[base + p, 1])
+        o_re, o_im = cut(own_ref, rim_ref, n, *spot(me_ref, corner_ref, base + p))
         patch_ref[p, 0] = o_re.astype(jnp.bfloat16)
         patch_ref[p, 1] = o_im.astype(jnp.bfloat16)
         q_re, q_im = probe_ref[0], probe_ref[1]
@@ -108,7 +128,7 @@
 
 
 def second_kernel(
-    corner_ref, own_ref, rim_ref, probe_ref, kernel_ref, first_ref, second_ref, patch_ref, moved_ref, *rest
+    me_ref, corner_ref, own_ref, rim_ref, probe_ref, kernel_ref, first_ref, second_ref, patch_ref, moved_ref, *rest
 ):
     measured_refs = rest[:-3]
     grad_ref, probe_grad_ref, measured_ref = rest[-3:]
@@ -123,7 +143,7 @@
 
     seconds, slabs = [], []
     for p in range(count):
-        o_re, o_im = cut(own_ref, rim_ref, n, corner_ref[base + p, 0], corner_ref[base + p, 1])
+        o_re, o_im = cut(own_ref, rim_ref, n, *spot(me_ref, corner_ref, base + p))
         m_re, m_im = moved_ref[p, 0], moved_ref[p, 1]
         slabs.append((o_re, o_im))
         seconds.append((m_re * o_re - m_im * o_im, m_re * o_im + m_im * o_re))
@@ -158,20 +178,25 @@
     probe_grad_ref[1] = total_im
 
 
-def place_kernel(corner_ref, grad_ref, slab_ref, part_ref, rim_ref):
+def placed_rows(me_ref, corner_ref, grad_ref, width, rows, first_row):
     positions, _, n, _ = grad_ref.shape
-    height, width = slab_ref.shape[1:]
-    wide = []
+    wide, tall = [], []
     for p in range(positions):
-        move = one_hot_rows((n, width), corner_ref[p, 1])
+        corner_y, corner_x = spot(me_ref, corner_ref, p)
+        move = one_hot_rows((n, width), corner_x)
         wide.append(product(grad_ref[p, 0], move).astype(jnp.bfloat16))
-    wide = jnp.concatenate(wide, 0)
-    tall = jnp.concatenate(
-        [one_hot_columns((height + n, n), corner_ref[p, 0]) for p in range(positions)], 1
-    )
-    total = product(tall, wide)
-    part_ref[0] = slab_ref[0] - step_object * total[:height]
-    rim_ref[0] = total[height:].astype(jnp.bfloat16)
+        tall.append(one_hot_columns((rows, n), corner_y - first_row))
+    return product(jnp.concatenate(tall, 1), jnp.concatenate(wide, 0))
+
+
+def place_rim_kernel(me_ref, corner_ref, grad_ref, rim_ref, *, height):
+    rows, width = rim_ref.shape[1:]
+    rim_ref[0] = placed_rows(me_ref, corner_ref, grad_ref, width, rows, height).astype(jnp.bfloat16)
+
+
+def place_own_kernel(me_ref, corner_ref, grad_ref, slab_ref, part_ref):
+    rows, width = part_ref.shape[1:]
+    part_ref[0] = slab_ref[0] - step_object * placed_rows(me_ref, corner_ref, grad_ref, width, rows, 0)
 
 
 def whole(shape):
@@ -222,22 +247,45 @@
     first, second = dft_tables(n)
     kernel = jnp.stack([jnp.cos(prop_phase), jnp.sin(prop_phase)], 0)
 
-    own = [object_slab[s].astype(jnp.bfloat16) for s in range(slice_count)]
-    rim = [from_behind(block[:, :n], "row", -1) for block in own]
-
-    sources = slot_source[:, 0]
-
-    def message(target):
-        hit = sources == target
-        chosen = lax.dynamic_index_in_dim(intensities, jnp.argmax(hit), 0, keepdims=False)
-        return jnp.where(jnp.any(hit), chosen, -1.0).astype(jnp.bfloat16)
-
-    measured = [message(me)]
-    origins = [me]
+    planes = slice_count * pair_count
+    slab = object_slab.reshape(planes, height, width)
+    params = pltpu.CompilerParams(vmem_limit_bytes=VMEM_BYTES)
+    me_array = jnp.reshape(me, (1,)).astype(jnp.int32)
+    spots = corners.reshape(row_count, 2)
+    sources = slot_source.reshape(slot_count)
+    smem = pl.BlockSpec(memory_space=pltpu.SMEM)
+    tile = (pair_count, height, width)
+    own_zero = pl.pallas_call(
+        first_prep_kernel,
+        grid=(pair_count,),
+        in_specs=[pl.BlockSpec((1, height, width), lambda i: (i, 0, 0))],
+        out_specs=pl.BlockSpec((1, height, width), lambda i: (i, 0, 0)),
+        out_shape=jax.ShapeDtypeStruct(tile, jnp.bfloat16),
+        compiler_params=params,
+        name="prepare_zero",
+    )(slab)
+    rim_zero = from_behind(own_zero[:, :n], "row", -1)
+    own_one, *messages = pl.pallas_call(
+        second_prep_kernel,
+        grid=(1,),
+        in_specs=[
+            smem,
+            smem,
+            pl.BlockSpec(tile, lambda i: (1, 0, 0)),
+            pl.BlockSpec(intensities.shape, lambda i: (0, 0, 0)),
+        ],
+        out_specs=[pl.BlockSpec(tile, lambda i: (0, 0, 0))]
+        + [pl.BlockSpec((n, n), lambda i: (0, 0))] * row_count,
+        out_shape=[jax.ShapeDtypeStruct(tile, jnp.bfloat16)]
+        + [jax.ShapeDtypeStruct((n, n), jnp.bfloat16)] * row_count,
+        compiler_params=params,
+        name="prepare_one",
+    )(me_array, sources, slab, intensities)
+    rim_one = from_behind(own_one[:, :n], "row", -1)
+    own, rim = [own_zero, own_one], [rim_zero, rim_one]
+    measured = [messages[0]]
     for s in range(1, row_count):
-        measured.append(permute_pairs(message(me ^ s), "row", lambda i: i ^ s))
-        origins.append(me ^ s)
-    spots = jnp.take(corners[:, 0], jnp.stack(origins), axis=0)
+        measured.append(permute_pairs(messages[s], "row", lambda i: i ^ s))
 
     count = 2
     steps = row_count // count
@@ -245,12 +293,11 @@
     patch_block = per_position((count, 2, n, n))
     table_specs = [whole((2 * n, 2 * n))] * 2
     tile_specs = [whole((pair_count, height, width)), whole((pair_count, n, width))]
-    params = pltpu.CompilerParams(vmem_limit_bytes=VMEM_BYTES)
     unit = 2 * n * n * n
     patches, moved = pl.pallas_call(
         first_kernel,
         grid_spec=pltpu.PrefetchScalarGridSpec(
-            num_scalar_prefetch=1,
+            num_scalar_prefetch=2,
             grid=(steps,),
             in_specs=tile_specs + [whole(plane)] * 2 + table_specs,
             out_specs=[patch_block, patch_block],
@@ -262,11 +309,11 @@
         compiler_params=params,
         cost_estimate=pl.CostEstimate(flops=row_count * 28 * unit, bytes_accessed=6 * 2**20, transcendentals=0),
         name="first_half",
-    )(spots, own[0], rim[0], probe_field, kernel, first, second)
+    )(me_array, spots, own[0], rim[0], probe_field, kernel, first, second)
     grads, probe_grad = pl.pallas_call(
         second_kernel,
         grid_spec=pltpu.PrefetchScalarGridSpec(
-            num_scalar_prefetch=1,
+            num_scalar_prefetch=2,
             grid=(steps,),
             in_specs=tile_specs
             + [whole(plane)] * 2
@@ -283,28 +330,26 @@
         compiler_params=params,
         cost_estimate=pl.CostEstimate(flops=row_count * 44 * unit, bytes_accessed=8 * 2**20, transcendentals=0),
         name="second_half",
-    )(spots, own[1], rim[1], probe_field, kernel, first, second, patches, moved, *measured)
-
-    planes = slice_count * pair_count
-    part, rim_grad = pl.pallas_call(
-        place_kernel,
-        grid_spec=pltpu.PrefetchScalarGridSpec(
-            num_scalar_prefetch=1,
-            grid=(planes,),
-            in_specs=[
-                pl.BlockSpec((row_count, 1, n, n), lambda i, *_: (0, i, 0, 0)),
-                per_position((1, height, width)),
-            ],
-            out_specs=[per_position((1, height, width)), per_position((1, n, width))],
-        ),
-        out_shape=[
-            jax.ShapeDtypeStruct((planes, height, width), jnp.float32),
-            jax.ShapeDtypeStruct((planes, n, width), jnp.bfloat16),
-        ],
-        compiler_params=params,
-        cost_estimate=pl.CostEstimate(flops=row_count * 24 * unit, bytes_accessed=7 * 2**20, transcendentals=0),
-        name="place",
-    )(spots, grads, object_slab.reshape(planes, height, width))
+    )(me_array, spots, own[1], rim[1], probe_field, kernel, first, second, patches, moved, *measured)
+
+    def place(body, block_rows, out_type, arrays, name):
+        extra = [per_position((1, height, width))] * len(arrays)
+        return pl.pallas_call(
+            body,
+            grid_spec=pltpu.PrefetchScalarGridSpec(
+                num_scalar_prefetch=2,
+                grid=(planes,),
+                in_specs=[pl.BlockSpec((row_count, 1, n, n), lambda i, *_: (0, i, 0, 0))] + extra,
+                out_specs=per_position((1, block_rows, width)),
+            ),
+            out_shape=jax.ShapeDtypeStruct((planes, block_rows, width), out_type),
+            compiler_params=params,
+            cost_estimate=pl.CostEstimate(flops=row_count * 16 * unit, bytes_accessed=4 * 2**20, transcendentals=0),
+            name=name,
+        )(me_array, spots, grads, *arrays)
+
+    rim_grad = place(functools.partial(place_rim_kernel, height=height), n, jnp.bfloat16, [], "place_rim")
+    part = place(place_own_kernel, height, jnp.float32, [slab], "place_own")
     total_probe = sum_everywhere(probe_grad.reshape(2 * n, n)).reshape(probe_field.shape)
     rim_grad = from_behind(rim_grad, "row", 1).astype(jnp.float32)
     updated_slab = part.at[:, :n].add(-step_object * rim_grad).reshape(object_slab.shape)

time: 88.3 us -> 71.3 us (0.81)
  other arithmetic: 19.4 us -> 6.7 us
  between operations: 8.31 us -> 0.87 us
  Pallas kernels: 25.8 us -> 29.4 us
  local copies, waits for them, and re-layouts: 3.34 us -> 6.91 us
  waiting for transfers between devices: 12.8 us -> 10.5 us
  starting transfers between devices: 18 us -> 16.5 us
    another operation x5 -> x0, other arithmetic: 7.07 us -> none  [the longest x4 5.34 us: message(): jnp.argmax(hit)]
    convert_element_type x1 -> x0, other arithmetic: 4.49 us -> none  [message(): return jnp.where(jnp.any(hit), chosen, -1.0).astype(jnp.bfloat16)]
    pallas_call x1 -> x4, Pallas kernels: 6.56 us -> 10.3 us  [the longest x2 8.72 us: place(): pl.pallas_call(body, grid_spec=pltpu.PrefetchScalarGridSpec(num_scalar_pr...]
    unnamed x8 -> x16, local copies, waits for them, and re-layouts: 1.6 us -> 4.91 us
    ppermute x10, waiting for transfers between devices: 12.8 us -> 10.5 us  [permute_pairs(): lax.ppermute(block, axis, [(i, partner(i)) for i in range(lax.axis_size(a...]
    reduce_or x1 -> x0, other arithmetic: 1.4 us -> none  [message(): return jnp.where(jnp.any(hit), chosen, -1.0).astype(jnp.bfloat16)]
    add x1, other arithmetic: 2.95 us -> 1.73 us  [per_device(): part.at[:, :n].add(-step_object * rim_grad).reshape(object_slab.shape)]
    ppermute x3, starting transfers between devices: 5.97 us -> 4.88 us  [from_behind(): return lax.ppermute(block, axis, route)]
  transfers between devices with their start and end apart: 13 -> 13, of which waited for: 6 -> 5; matrix products, arithmetic and copies ran while one was open for 8% -> 10% of each run, Pallas kernels for 16% -> 25%
where the time goes in v1:
time: 71.3 us; the launch traced here: 70.8 us
  Pallas kernels  29.4 us (41%)
  starting transfers between devices  16.5 us (23%)
  waiting for transfers between devices  10.5 us (15%)
  local copies, waits for them, and re-layouts  6.91 us (10%)
  other arithmetic  6.7 us (9%)
  between operations  0.87 us (1%)
    ppermute x10, starting transfers between devices, permute_pairs(): lax.ppermute(block, axis, [(i, partner(i)) for i in range(lax.axis_size(a...  11.6 us
    pallas_call x1, Pallas kernels, per_device(): pl.pallas_call(second_kernel, grid_spec=pltpu.PrefetchScalarGridSpec(num_...  11.5 us
    ppermute x10, waiting for transfers between devices, permute_pairs(): lax.ppermute(block, axis, [(i, partner(i)) for i in range(lax.axis_size(a...  10.5 us
    pallas_call x2, Pallas kernels, place(): pl.pallas_call(body, grid_spec=pltpu.PrefetchScalarGridSpec(num_scalar_pr...  8.72 us
    pallas_call x1, Pallas kernels, per_device(): pl.pallas_call(first_kernel, grid_spec=pltpu.PrefetchScalarGridSpec(num_s...  7.67 us
    unnamed x16, local copies, waits for them, and re-layouts  4.91 us
    ppermute x3, starting transfers between devices, from_behind(): return lax.ppermute(block, axis, route)  4.88 us
    another operation x1, local copies, waits for them, and re-layouts, per_device(): kernel = jnp.stack([jnp.cos(prop_phase), jnp.sin(prop_phase)], 0)  1.85 us
  transfers between devices with their start and end apart: 13, of which 5 were waited for; matrix products, arithmetic and copies ran while one was open for 10% of the time, Pallas kernels for 25%

profile of v1, /device:TPU:0, one launch (start us, length us, event | category | flops | bytes accessed | tf_op | source)
XLA Modules:
  0.0 70.8 jit_solution(14289006928000071762)
XLA Ops:
  0.6 0.0 copy-start.4
  0.6 0.0 copy-start
  0.7 1.6 %copy-done = f32[2,2,256,512]{3,2,1,0:T(8,128)S(1)} copy-done((f32[2,2,256,512]{3,2,1,0:T(8,128)S(1)}, f32[2,2,256,512]{3,2,1,0:T(8,128)}, u32[]{:S(2)}) %copy-start) | copy-done | bytes 2097176
  2.2 0.0 copy-start.1
  2.2 0.0 copy-start.2
  2.2 0.1 prepare_zero.1.own_ref
  2.3 1.4 %collective-permute-start.1 = (bf16[2,256,512]{2,1,0:T(8,128)(2,1)S(1)}, bf16[2,256,512]{2,1,0:T(8,128)(2,1)}, u32[]{:S(2)}, u32[]{:S(2)}) collective-permute-start(bf16[2,256,512]{2,1,0:T(8,128)(2,1)S(1)} %prepare_zero.1.own_ref), channel_id=1, source_target_pairs={{4,0},{8,4},{12,8},{5,1},{9,5},{13,9},{6,2},{10,6},{14,10},{7,3},{... | collective-permute-start | bytes 1572872 | tf_op jit(solution)/shard_map/ppermute | solution.py:22
  3.8 0.0 copy-done.4
  3.8 0.1 copy-done.1
  3.8 0.1 copy-done.2
  3.9 0.0 copy-start.7
  3.9 1.5 %prepare_one.1 = (bf16[2,256,512]{2,1,0:T(8,128)(2,1)}, bf16[256,256]{1,0:T(8,128)(2,1)S(1)}, bf16[256,256]{1,0:T(8,128)(2,1)}, bf16[256,256]{1,0:T(8,128)(2,1)S(1)}, bf16[256,256]{1,0:T(8,128)(2,1)S(1)}) custom-call(s32[1]{0:T(128)} %bitcast.me_ref, s32[2]{0:T(128)S(1)} %bitcast.16, f32[4,256,512]{2,1,0:T(8,128)S(1)} %bitcast.13, f32[2,256,256]{2,1,0:T(8,128)S(1)} %copy-done.2), custom_call_target="tpu_custom_call" | custom-call | tf_op jit(solution)/shard_map/prepare_one/pallas_call | solution.py:268
  5.4 0.0 copy-start.3
  5.4 1.4 %collective-permute-start = (bf16[2,256,512]{2,1,0:T(8,128)(2,1)}, bf16[2,256,512]{2,1,0:T(8,128)(2,1)S(1)}, u32[]{:S(2)}, u32[]{:S(2)}) collective-permute-start(bf16[2,256,512]{2,1,0:T(8,128)(2,1)} %get-tuple-element.31.own_ref), channel_id=1, source_target_pairs={{4,0},{8,4},{12,8},{5,1},{9,5},{13,9},{6,2},{10,6},{14,10},{7,3},{... | collective-permute-start | bytes 1572872 | tf_op jit(solution)/shard_map/ppermute | solution.py:22
  6.8 1.7 %collective-permute-start.2 = (bf16[256,256]{1,0:T(8,128)(2,1)}, bf16[256,256]{1,0:T(8,128)(2,1)S(1)}, u32[]{:S(2)}, u32[]{:S(2)}) collective-permute-start(bf16[256,256]{1,0:T(8,128)(2,1)} %get-tuple-element.35), channel_id=1, source_target_pairs={{0,4},{4,0},{8,12},{12,8},{1,5},{5,1},{9,13},{13,9},{2,6},{6,2},{1... | collective-permute-start | bytes 393224 | tf_op jit(solution)/shard_map/ppermute | solution.py:16
  8.5 3.1 %collective-permute-start.3 = (bf16[256,256]{1,0:T(8,128)(2,1)S(1)}, bf16[256,256]{1,0:T(8,128)(2,1)S(1)}, u32[]{:S(2)}, u32[]{:S(2)}) collective-permute-start(bf16[256,256]{1,0:T(8,128)(2,1)S(1)} %get-tuple-element.36), channel_id=1, source_target_pairs={{0,8},{4,12},{8,0},{12,4},{1,9},{5,13},{9,1},{13,5},{2,10},{6,14},... | collective-permute-start | bytes 393224 | tf_op jit(solution)/shard_map/ppermute | solution.py:16
  11.6 0.0 collective-permute-start.4
  11.6 1.9 %cosine_bitcast_fusion = (f32[1,256,256]{2,1,0:T(8,128)S(1)}, f32[1,256,256]{2,1,0:T(8,128)S(1)}) fusion(f32[256,256]{1,0:T(8,128)} %param.12), kind=kLoop, calls=%fused_computation.22 | loop fusion | bytes 786432 | tf_op jit(solution)/shard_map/stack | solution.py:248
  13.5 1.8 %multiply_convert_fusion = (bf16[256,256]{1,0:T(8,128)(2,1)}, bf16[256,256]{1,0:T(8,128)(2,1)}) fusion(), kind=kLoop, calls=%fused_computation.17 | loop fusion | flops 1245184 | bytes 262144 | tf_op jit(solution)/shard_map/convert_element_type | solution.py:31
  15.3 1.0 %fusion.9 = bf16[256,256]{1,0:T(8,128)(2,1)S(1)} fusion(), kind=kLoop, calls=%fused_computation.30 | loop fusion | flops 1310720 | bytes 131072 | tf_op jit(solution)/shard_map/neg | solution.py:33
  16.3 0.0 copy-done.7
  16.3 0.1 copy.10.corner_ref
  16.4 1.2 %fusion.1 = (bf16[512,512]{1,0:T(8,128)(2,1)S(1)}, bf16[512,512]{1,0:T(8,128)(2,1)S(1)}) fusion(bf16[256,256]{1,0:T(8,128)(2,1)} %get-tuple-element.49, bf16[256,256]{1,0:T(8,128)(2,1)S(1)} %fusion.9, bf16[256,256]{1,0:T(8,128)(2,1)} %get-tuple-element.48), kind=kLoop, calls=%fused_computation.6 | loop fusion | flops 3670016 | bytes 1441792 | tf_op jit(solution)/shard_map/concatenate | solution.py:35
  17.6 0.0 collective-permute-done.1.rim_ref
  17.6 0.0 copy-done.3
  17.6 7.7 %first_half.1 = (bf16[4,2,256,256]{3,2,1,0:T(8,128)(2,1)S(1)}, f32[4,2,256,256]{3,2,1,0:T(8,128)}) custom-call(s32[1]{0:T(128)} %bitcast.me_ref, s32[4,2]{1,0:T(4,128)S(1)} %copy.10.corner_ref, bf16[2,256,512]{2,1,0:T(8,128)(2,1)S(1)} %prepare_zero.1.own_ref, bf16[2,256,512]{2,1,0:T(8,128)(2,1)} %collective-permute-done.1.rim_ref, ...), custom_call_target="tpu_custom_call" | custom-call | flops 3758096384 | bytes 6291456 | tf_op jit(solution)/shard_map/first_half/pallas_call | solution.py:297
  25.3 0.0 collective-permute-done.2.rest_1_
  25.3 0.0 collective-permute-done.3.rest_2_
  25.3 0.0 collective-permute-done.4.rest_3_
  25.3 0.0 collective-permute-done.rim_ref
  25.3 11.5 %second_half.1 = (bf16[4,4,256,256]{3,2,1,0:T(8,128)(2,1)}, f32[2,256,256]{2,1,0:T(8,128)S(1)}) custom-call(s32[1]{0:T(128)} %bitcast.me_ref, s32[4,2]{1,0:T(4,128)S(1)} %copy.10.corner_ref, bf16[2,256,512]{2,1,0:T(8,128)(2,1)} %get-tuple-element.31.own_ref, bf16[2,256,512]{2,1,0:T(8,128)(2,1)S(1)} %collective-permute-done.rim_ref, ...), custom_call_target="tpu_custom_call" | custom-call | flops 5905580032 | bytes 8388608 | tf_op jit(solution)/shard_map/second_half/pallas_call | solution.py:313
  36.8 0.3 collective-permute-start.6
  37.1 1.1 %collective-permute-done.6 = bf16[256,256]{1,0:T(8,128)(2,1)S(1)} collective-permute-done((bf16[256,256]{1,0:T(8,128)(2,1)S(1)}, bf16[256,256]{1,0:T(8,128)(2,1)S(1)}, u32[]{:S(2)}, u32[]{:S(2)}) %collective-permute-start.6) | collective-permute-done | bytes 131104 | tf_op jit(solution)/shard_map/ppermute | solution.py:16
  38.2 1.9 %collective-permute-start.7 = (bf16[128,256]{1,0:T(8,128)(2,1)S(1)}, bf16[128,256]{1,0:T(8,128)(2,1)S(1)}, u32[]{:S(2)}, u32[]{:S(2)}) collective-permute-start(bf16[128,256]{1,0:T(8,128)(2,1)S(1)} %dynamic-slice_convert_fusion.1), channel_id=1, source_target_pairs={{0,8},{4,12},{8,0},{12,4},{1,9},{5,13},{9,1},{13,5},{2,10},{6,14},... | collective-permute-start | bytes 196616 | tf_op jit(solution)/shard_map/ppermute | solution.py:16
  40.1 0.0 copy-start.5
  40.1 1.6 %copy-done.5 = bf16[4,4,256,256]{3,2,1,0:T(8,128)(2,1)S(1)} copy-done((bf16[4,4,256,256]{3,2,1,0:T(8,128)(2,1)S(1)}, bf16[4,4,256,256]{3,2,1,0:T(8,128)(2,1)}, u32[]{:S(2)}) %copy-start.5) | copy-done | bytes 2097176
  41.7 3.7 %place_rim.1 = bf16[4,256,512]{2,1,0:T(8,128)(2,1)S(1)} custom-call(s32[1]{0:T(128)} %bitcast.me_ref, s32[4,2]{1,0:T(4,128)S(1)} %copy.10.corner_ref, bf16[4,4,256,256]{3,2,1,0:T(8,128)(2,1)S(1)} %copy-done.5), custom_call_target="tpu_custom_call" | custom-call | flops 2147483648 | bytes 4194304 | tf_op jit(solution)/shard_map/place_rim/pallas_call | solution.py:337
  45.4 2.0 %collective-permute-start.5 = (bf16[4,256,512]{2,1,0:T(8,128)(2,1)S(1)}, bf16[4,256,512]{2,1,0:T(8,128)(2,1)S(1)}, u32[]{:S(2)}, u32[]{:S(2)}) collective-permute-start(bf16[4,256,512]{2,1,0:T(8,128)(2,1)S(1)} %place_rim.1), channel_id=1, source_target_pairs={{0,4},{4,8},{8,12},{1,5},{5,9},{9,13},{2,6},{6,10},{10,14},{3,7},{... | collective-permute-start | bytes 3145736 | tf_op jit(solution)/shard_map/ppermute | solution.py:22
  47.4 0.0 collective-permute-done.7
  47.5 3.7 %collective-permute-start.10 = (bf16[128,256]{1,0:T(8,128)(2,1)S(1)}, bf16[128,256]{1,0:T(8,128)(2,1)S(1)}, u32[]{:S(2)}, u32[]{:S(2)}) collective-permute-start(bf16[128,256]{1,0:T(8,128)(2,1)S(1)} %fusion.8), channel_id=1, source_target_pairs={{0,3},{1,2},{2,1},{3,0},{4,7},{5,6},{6,5},{7,4},{8,11},{9,10},{10,... | collective-permute-start | bytes 196616 | tf_op jit(solution)/shard_map/ppermute | solution.py:16
  51.2 0.0 collective-permute-start.8
  51.2 0.8 %collective-permute-start.9 = (bf16[128,256]{1,0:T(8,128)(2,1)S(1)}, bf16[128,256]{1,0:T(8,128)(2,1)S(1)}, u32[]{:S(2)}, u32[]{:S(2)}) collective-permute-start(bf16[128,256]{1,0:T(8,128)(2,1)S(1)} %fusion.8), channel_id=1, source_target_pairs={{0,2},{1,3},{2,0},{3,1},{4,6},{5,7},{6,4},{7,5},{8,10},{9,11},{10,... | collective-permute-start | bytes 196616 | tf_op jit(solution)/shard_map/ppermute | solution.py:16
  51.9 2.3 %collective-permute-done.10 = bf16[128,256]{1,0:T(8,128)(2,1)S(1)} collective-permute-done((bf16[128,256]{1,0:T(8,128)(2,1)S(1)}, bf16[128,256]{1,0:T(8,128)(2,1)S(1)}, u32[]{:S(2)}, u32[]{:S(2)}) %collective-permute-start.10) | collective-permute-done | bytes 65568 | tf_op jit(solution)/shard_map/ppermute | solution.py:16
  54.2 2.2 %collective-permute-done.8 = bf16[128,256]{1,0:T(8,128)(2,1)S(1)} collective-permute-done((bf16[128,256]{1,0:T(8,128)(2,1)S(1)}, bf16[128,256]{1,0:T(8,128)(2,1)S(1)}, u32[]{:S(2)}, u32[]{:S(2)}) %collective-permute-start.8) | collective-permute-done | bytes 65568 | tf_op jit(solution)/shard_map/ppermute | solution.py:16
  56.5 0.6 collective-permute-done.9
  57.1 0.1 collective-permute-start.11
  57.2 4.2 %collective-permute-done.11 = bf16[128,256]{1,0:T(8,128)(2,1)S(1)} collective-permute-done((bf16[128,256]{1,0:T(8,128)(2,1)S(1)}, bf16[128,256]{1,0:T(8,128)(2,1)S(1)}, u32[]{:S(2)}, u32[]{:S(2)}) %collective-permute-start.11) | collective-permute-done | bytes 65568 | tf_op jit(solution)/shard_map/ppermute | solution.py:16
  61.4 0.1 collective-permute-start.12
  61.5 0.0 copy-start.6
  61.5 1.6 %copy-done.6 = bf16[4,4,256,256]{3,2,1,0:T(8,128)(2,1)S(1)} copy-done((bf16[4,4,256,256]{3,2,1,0:T(8,128)(2,1)S(1)}, bf16[4,4,256,256]{3,2,1,0:T(8,128)(2,1)}, u32[]{:S(2)}) %copy-start.6) | copy-done | bytes 2097176
  63.1 5.0 %place_own.1 = f32[4,256,512]{2,1,0:T(8,128)S(1)} custom-call(s32[1]{0:T(128)} %bitcast.me_ref, s32[4,2]{1,0:T(4,128)S(1)} %copy.10.corner_ref, bf16[4,4,256,256]{3,2,1,0:T(8,128)(2,1)S(1)} %copy-done.6, f32[4,256,512]{2,1,0:T(8,128)} %bitcast.11), custom_call_target="tpu_custom_call" | custom-call | flops 2147483648 | bytes 4194304 | tf_op jit(solution)/shard_map/place_own/pallas_call | solution.py:337
  68.1 0.0 collective-permute-done.12
  68.2 0.9 %sub.12 = f32[2,256,256]{2,1,0:T(8,128)} subtract(f32[2,256,256]{2,1,0:T(8,128)S(1)} %copy-done.3, f32[2,256,256]{2,1,0:T(8,128)S(1)} %bitcast.17) | non-fusion elementwise | flops 131072 | bytes 1572864 | tf_op jit(solution)/shard_map/sub | solution.py:356
  69.1 0.0 collective-permute-done.5
  69.1 1.7 %multiply_add_fusion = f32[4,256,512]{2,1,0:T(8,128)} fusion(f32[4,256,512]{2,1,0:T(8,128)S(1)} %place_own.1, bf16[4,256,512]{2,1,0:T(8,128)(2,1)S(1)} %collective-permute-done.5), kind=kLoop, calls=%fused_computation | loop fusion | flops 1572864 | bytes 5242880 | tf_op jit(solution)/shard_map/add | solution.py:355
  (10 shorter events, 0.3 us)
Async XLA Ops:
  0.6 3.1 %copy-start.4 = (s32[2,1]{0,1:T(1,128)S(1)}, s32[2,1]{0,1:T(1,128)}, u32[]{:S(2)}) copy-start(s32[2,1]{0,1:T(1,128)} %param.15) | copy-start | bytes 28
  0.6 1.6 %copy-start = (f32[2,2,256,512]{3,2,1,0:T(8,128)S(1)}, f32[2,2,256,512]{3,2,1,0:T(8,128)}, u32[]{:S(2)}) copy-start(f32[2,2,256,512]{3,2,1,0:T(8,128)} %param.10) | copy-start | bytes 6291460
  2.2 1.6 %copy-start.1 = (f32[2,2,256,512]{3,2,1,0:T(8,128)S(1)}, f32[2,2,256,512]{3,2,1,0:T(8,128)}, u32[]{:S(2)}) copy-start(f32[2,2,256,512]{3,2,1,0:T(8,128)} %param.10) | copy-start | bytes 6291460
  2.2 1.7 %copy-start.2 = (f32[2,256,256]{2,1,0:T(8,128)S(1)}, f32[2,256,256]{2,1,0:T(8,128)}, u32[]{:S(2)}) copy-start(f32[2,256,256]{2,1,0:T(8,128)} %intensity_ref.1) | copy-start | bytes 1572868
  2.3 15.2 %collective-permute-start.1 = (bf16[2,256,512]{2,1,0:T(8,128)(2,1)S(1)}, bf16[2,256,512]{2,1,0:T(8,128)(2,1)}, u32[]{:S(2)}, u32[]{:S(2)}) collective-permute-start(bf16[2,256,512]{2,1,0:T(8,128)(2,1)S(1)} %prepare_zero.1.own_ref), channel_id=1, source_target_pairs={{4,0},{8,4},{12,8},{5,1},{9,5},{13,9},{6,2},{10,6},{14,10},{7,3},{... | collective-permute-start | bytes 1572872 | tf_op jit(solution)/shard_map/ppermute | solution.py:22
  3.9 12.4 %copy-start.7 = (s32[4,1,2]{0,2,1:T(2,128)S(1)}, s32[4,1,2]{0,2,1:T(2,128)}, u32[]{:S(2)}) copy-start(s32[4,1,2]{0,2,1:T(2,128)} %param.14) | copy-start | bytes 100
  5.4 12.2 %copy-start.3 = (f32[2,256,256]{2,1,0:T(8,128)S(1)}, f32[2,256,256]{2,1,0:T(8,128)}, u32[]{:S(2)}) copy-start(f32[2,256,256]{2,1,0:T(8,128)} %probe_ref.3) | copy-start | bytes 1572868
  5.4 19.9 %collective-permute-start = (bf16[2,256,512]{2,1,0:T(8,128)(2,1)}, bf16[2,256,512]{2,1,0:T(8,128)(2,1)S(1)}, u32[]{:S(2)}, u32[]{:S(2)}) collective-permute-start(bf16[2,256,512]{2,1,0:T(8,128)(2,1)} %get-tuple-element.31.own_ref), channel_id=1, source_target_pairs={{4,0},{8,4},{12,8},{5,1},{9,5},{13,9},{6,2},{10,6},{14,10},{7,3},{... | collective-permute-start | bytes 1572872 | tf_op jit(solution)/shard_map/ppermute | solution.py:22
  6.8 18.5 %collective-permute-start.2 = (bf16[256,256]{1,0:T(8,128)(2,1)}, bf16[256,256]{1,0:T(8,128)(2,1)S(1)}, u32[]{:S(2)}, u32[]{:S(2)}) collective-permute-start(bf16[256,256]{1,0:T(8,128)(2,1)} %get-tuple-element.35), channel_id=1, source_target_pairs={{0,4},{4,0},{8,12},{12,8},{1,5},{5,1},{9,13},{13,9},{2,6},{6,2},{1... | collective-permute-start | bytes 393224 | tf_op jit(solution)/shard_map/ppermute | solution.py:16
  8.5 16.7 %collective-permute-start.3 = (bf16[256,256]{1,0:T(8,128)(2,1)S(1)}, bf16[256,256]{1,0:T(8,128)(2,1)S(1)}, u32[]{:S(2)}, u32[]{:S(2)}) collective-permute-start(bf16[256,256]{1,0:T(8,128)(2,1)S(1)} %get-tuple-element.36), channel_id=1, source_target_pairs={{0,8},{4,12},{8,0},{12,4},{1,9},{5,13},{9,1},{13,5},{2,10},{6,14},... | collective-permute-start | bytes 393224 | tf_op jit(solution)/shard_map/ppermute | solution.py:16
  11.6 13.6 %collective-permute-start.4 = (bf16[256,256]{1,0:T(8,128)(2,1)S(1)}, bf16[256,256]{1,0:T(8,128)(2,1)S(1)}, u32[]{:S(2)}, u32[]{:S(2)}) collective-permute-start(bf16[256,256]{1,0:T(8,128)(2,1)S(1)} %get-tuple-element.37), channel_id=1, source_target_pairs={{0,12},{4,8},{8,4},{12,0},{1,13},{5,9},{9,5},{13,1},{2,14},{6,10},... | collective-permute-start | bytes 393224 | tf_op jit(solution)/shard_map/ppermute | solution.py:16
  36.8 1.4 %collective-permute-start.6 = (bf16[256,256]{1,0:T(8,128)(2,1)S(1)}, bf16[256,256]{1,0:T(8,128)(2,1)S(1)}, u32[]{:S(2)}, u32[]{:S(2)}) collective-permute-start(bf16[256,256]{1,0:T(8,128)(2,1)S(1)} %dynamic-slice_convert_fusion), channel_id=1, source_target_pairs={{0,4},{4,0},{8,12},{12,8},{1,5},{5,1},{9,13},{13,9},{2,6},{6,2},{1... | collective-permute-start | bytes 393224 | tf_op jit(solution)/shard_map/ppermute | solution.py:16
  38.2 9.2 %collective-permute-start.7 = (bf16[128,256]{1,0:T(8,128)(2,1)S(1)}, bf16[128,256]{1,0:T(8,128)(2,1)S(1)}, u32[]{:S(2)}, u32[]{:S(2)}) collective-permute-start(bf16[128,256]{1,0:T(8,128)(2,1)S(1)} %dynamic-slice_convert_fusion.1), channel_id=1, source_target_pairs={{0,8},{4,12},{8,0},{12,4},{1,9},{5,13},{9,1},{13,5},{2,10},{6,14},... | collective-permute-start | bytes 196616 | tf_op jit(solution)/shard_map/ppermute | solution.py:16
  40.1 1.6 %copy-start.5 = (bf16[4,4,256,256]{3,2,1,0:T(8,128)(2,1)S(1)}, bf16[4,4,256,256]{3,2,1,0:T(8,128)(2,1)}, u32[]{:S(2)}) copy-start(bf16[4,4,256,256]{3,2,1,0:T(8,128)(2,1)} %get-tuple-element.38.grad_ref) | copy-start | bytes 6291460
  45.4 23.7 %collective-permute-start.5 = (bf16[4,256,512]{2,1,0:T(8,128)(2,1)S(1)}, bf16[4,256,512]{2,1,0:T(8,128)(2,1)S(1)}, u32[]{:S(2)}, u32[]{:S(2)}) collective-permute-start(bf16[4,256,512]{2,1,0:T(8,128)(2,1)S(1)} %place_rim.1), channel_id=1, source_target_pairs={{0,4},{4,8},{8,12},{1,5},{5,9},{9,13},{2,6},{6,10},{10,14},{3,7},{... | collective-permute-start | bytes 3145736 | tf_op jit(solution)/shard_map/ppermute | solution.py:22
  47.5 6.8 %collective-permute-start.10 = (bf16[128,256]{1,0:T(8,128)(2,1)S(1)}, bf16[128,256]{1,0:T(8,128)(2,1)S(1)}, u32[]{:S(2)}, u32[]{:S(2)}) collective-permute-start(bf16[128,256]{1,0:T(8,128)(2,1)S(1)} %fusion.8), channel_id=1, source_target_pairs={{0,3},{1,2},{2,1},{3,0},{4,7},{5,6},{6,5},{7,4},{8,11},{9,10},{10,... | collective-permute-start | bytes 196616 | tf_op jit(solution)/shard_map/ppermute | solution.py:16
  51.2 5.3 %collective-permute-start.8 = (bf16[128,256]{1,0:T(8,128)(2,1)S(1)}, bf16[128,256]{1,0:T(8,128)(2,1)S(1)}, u32[]{:S(2)}, u32[]{:S(2)}) collective-permute-start(bf16[128,256]{1,0:T(8,128)(2,1)S(1)} %fusion.8), channel_id=1, source_target_pairs={{0,1},{1,0},{2,3},{3,2},{4,5},{5,4},{6,7},{7,6},{8,9},{9,8},{10,11... | collective-permute-start | bytes 196616 | tf_op jit(solution)/shard_map/ppermute | solution.py:16
  51.2 5.9 %collective-permute-start.9 = (bf16[128,256]{1,0:T(8,128)(2,1)S(1)}, bf16[128,256]{1,0:T(8,128)(2,1)S(1)}, u32[]{:S(2)}, u32[]{:S(2)}) collective-permute-start(bf16[128,256]{1,0:T(8,128)(2,1)S(1)} %fusion.8), channel_id=1, source_target_pairs={{0,2},{1,3},{2,0},{3,1},{4,6},{5,7},{6,4},{7,5},{8,10},{9,11},{10,... | collective-permute-start | bytes 196616 | tf_op jit(solution)/shard_map/ppermute | solution.py:16
  57.1 4.3 %collective-permute-start.11 = (bf16[128,256]{1,0:T(8,128)(2,1)S(1)}, bf16[128,256]{1,0:T(8,128)(2,1)S(1)}, u32[]{:S(2)}, u32[]{:S(2)}) collective-permute-start(bf16[128,256]{1,0:T(8,128)(2,1)S(1)} %get-tuple-element.41), channel_id=1, source_target_pairs={{0,8},{4,12},{8,0},{12,4},{1,9},{5,13},{9,1},{13,5},{2,10},{6,14},... | collective-permute-start | bytes 196616 | tf_op jit(solution)/shard_map/ppermute | solution.py:16
  61.4 6.7 %collective-permute-start.12 = (bf16[256,256]{1,0:T(8,128)(2,1)S(1)}, bf16[256,256]{1,0:T(8,128)(2,1)S(1)}, u32[]{:S(2)}, u32[]{:S(2)}) collective-permute-start(bf16[256,256]{1,0:T(8,128)(2,1)S(1)} %constant_dynamic-update-slice_fusion), channel_id=1, source_target_pairs={{0,4},{4,0},{8,12},{12,8},{1,5},{5,1},{9,13},{13,9},{2,6},{6,2},{1... | collective-permute-start | bytes 393224 | tf_op jit(solution)/shard_map/ppermute | solution.py:16
  61.5 1.6 %copy-start.6 = (bf16[4,4,256,256]{3,2,1,0:T(8,128)(2,1)S(1)}, bf16[4,4,256,256]{3,2,1,0:T(8,128)(2,1)}, u32[]{:S(2)}) copy-start(bf16[4,4,256,256]{3,2,1,0:T(8,128)(2,1)} %get-tuple-element.38.grad_ref) | copy-start | bytes 6291460
